TPU v7x, 256 devices: a whole 4x4x8 slice. The times are simulated.
256 devices in a mesh: ctx: 64 (over z, x, core), head: 4 (over y).
Axes of the slice: x: 4, y: 4, z: 8, core: 2. Of those that a mesh axis runs over, the one named last changes fastest.
Arguments:
- queries: bfloat16 [12288, 16384], P('ctx', 'head'), may hold values from -16 to 16
- keys: bfloat16 [12288, 1024], P('ctx', 'head'), may hold values from -16 to 16
- values: bfloat16 [12288, 1024], P('ctx', 'head'), may hold values from -6 to 6
- doc_lengths: int32 [128], replicated, may hold values from 1 to 2880, 12288 in all
Outputs:
- attended: bfloat16 [12288, 16384], P(('ctx', 'head'))
Inputs may be any that keep to these rules, and one draw needn't show every extreme that they name: `doc_lengths`: the longest document has exactly 2880 tokens.
All inputs are finite; a program needn't handle non-finite values.
Results may differ from a plain program's by a relative error of at most 0.0029.
Values may be sent and summed in bfloat16 or wider, within the bound.
A program may use at most 64 MiB of HBM per device.

v0:
```python
import jax
import jax.numpy as jnp
from jax import lax
from jax.sharding import PartitionSpec as P

HEAD_SIZE = 128


def passed_along(value, axis, steps):
    count = lax.axis_size(axis)
    leading, last = (max(0, -steps), min(count, count - steps))
    return lax.ppermute(value, axis, [(source, source + steps) for source in range(leading, last)])


def attend_group(query_part, key_part, value_part, allowed):
    scores = jnp.einsum(
        "qhd,kd->hqk", query_part, key_part, preferred_element_type=jnp.float32
    ) * HEAD_SIZE ** (-0.5)
    scores = jnp.where(allowed[None], scores, -1e30)
    highest = jnp.max(scores, axis=-1, keepdims=True)
    probs = jnp.where(allowed[None], jnp.exp(scores - highest), 0.0)
    totals = jnp.sum(probs, axis=-1)
    rounded = probs.astype(jnp.bfloat16)
    mixed = jnp.einsum("hqk,kd->qhd", rounded, value_part, preferred_element_type=jnp.float32)
    return (mixed / jnp.transpose(totals)[:, :, None]).astype(jnp.bfloat16)


def document_ids(doc_ends, positions):
    return jnp.sum((doc_ends[None, :] <= positions[:, None]).astype(jnp.int32), axis=1)


def per_device(queries, keys, values, doc_lengths):
    tok_rows = queries.shape[0]
    width_of_keys = keys.shape[1]
    hop_count = lax.axis_size("ctx") // 4
    ctx_place = lax.axis_index("ctx")
    own_block = jnp.stack([keys, values])
    window = jnp.concatenate(
        [jnp.zeros((2, (hop_count - 1) * tok_rows, width_of_keys), own_block.dtype), own_block],
        axis=1,
    )

    def relay_step(hop_index, carry_pair):
        collected, moving = carry_pair
        moving = passed_along(moving, "ctx", 1)
        slot_start = (hop_count - 2 - hop_index) * tok_rows
        collected = lax.dynamic_update_slice_in_dim(collected, moving, slot_start, 1)
        return (collected, moving)

    window, moving = lax.fori_loop(0, hop_count - 1, relay_step, (window, own_block))
    doc_ends = jnp.cumsum(doc_lengths)
    query_pos = ctx_place * tok_rows + jnp.arange(tok_rows, dtype=jnp.int32)
    key_pos = (ctx_place - hop_count + 1) * tok_rows + jnp.arange(
        hop_count * tok_rows, dtype=jnp.int32
    )
    query_docs = document_ids(doc_ends, query_pos)
    key_docs = jnp.where(key_pos >= 0, document_ids(doc_ends, key_pos), -1)
    allowed = (key_docs[None, :] == query_docs[:, None]) & (key_pos[None, :] <= query_pos[:, None])
    groups = width_of_keys // HEAD_SIZE
    per_group = queries.shape[1] // HEAD_SIZE // groups
    heads_item = 4
    item_count = groups * per_group // heads_item
    query_items = jnp.moveaxis(queries.reshape(tok_rows, item_count, heads_item, HEAD_SIZE), 1, 0)
    key_heads = window[0].reshape(hop_count * tok_rows, groups, HEAD_SIZE)
    value_heads = window[1].reshape(hop_count * tok_rows, groups, HEAD_SIZE)

    def one_item(item_index):
        group_index = item_index // (per_group // heads_item)
        return attend_group(
            query_items[item_index], key_heads[:, group_index], value_heads[:, group_index], allowed
        )

    mixed = lax.map(one_item, jnp.arange(item_count, dtype=jnp.int32))
    mixed = jnp.moveaxis(mixed, 0, 1).reshape(tok_rows, item_count * heads_item * HEAD_SIZE)
    return lax.all_to_all(mixed, "head", split_axis=0, concat_axis=1, tiled=True)


def solution(mesh):
    placed = (P("ctx", "head"), P("ctx", "head"), P("ctx", "head"), P())
    return jax.shard_map(
        per_device, mesh=mesh, in_specs=placed, out_specs=P(("ctx", "head"), None), check_vma=False
    )
```

profile of v0, /device:TPU:128, one launch (start us, length us, event | category | flops | bytes accessed | tf_op | source)
XLA Modules:
  0.0 334.9 jit_solution(958149482969775816)
XLA Ops:
  0.0 0.8 copy.23
  1.0 1.9 convert_reduce_fusion
  3.5 1.0 pad_maximum_fusion
  4.7 155.5 %while.28 = (s32[]{:T(128)}, bf16[2,3072,256]{2,1,0:T(8,128)(2,1)S(1)}, bf16[2,192,256]{2,1,0:T(8,128)(2,1)S(1)}, s32[]{:T(128)}, s32[]{:T(128)}, /*index=5*/s32[]{:T(128)}, s32[]{:T(128)}, s32[]{:T(128)}) while((s32[]{:T(128)}, bf16[2,3072,256]{2,1,0:T(8,128)(2,1)S(1)}, bf16[2,192,256]{2,1,0:T(8,128)(2,1)S(1)}, s32[]{:T(128)}, s32[]{:T(128)}, ...), condition=%wide.region_1.0_spmd, body=%wide.region_0.0_spmd.sunk | while | flops 7 | bytes 1573051 | solution.py:50
  4.7 1.9 collective-permute-start
  6.7 8.4 %collective-permute-done = bf16[2,192,256]{2,1,0:T(8,128)(2,1)S(1)} collective-permute-done((bf16[2,192,256]{2,1,0:T(8,128)(2,1)S(1)}, bf16[2,192,256]{2,1,0:T(8,128)(2,1)S(1)}, u32[]{:S(2)}, u32[]{:S(2)}) %collective-permute-start) | collective-permute-done | bytes 196640 | tf_op jit(solution)/shard_map/while/body/eval_jaxpr/ppermute | solution.py:12
  15.1 1.9 collective-permute-start
  17.0 8.4 %collective-permute-done = bf16[2,192,256]{2,1,0:T(8,128)(2,1)S(1)} collective-permute-done((bf16[2,192,256]{2,1,0:T(8,128)(2,1)S(1)}, bf16[2,192,256]{2,1,0:T(8,128)(2,1)S(1)}, u32[]{:S(2)}, u32[]{:S(2)}) %collective-permute-start) | collective-permute-done | bytes 196640 | tf_op jit(solution)/shard_map/while/body/eval_jaxpr/ppermute | solution.py:12
  25.5 1.9 collective-permute-start
  27.4 8.4 %collective-permute-done = bf16[2,192,256]{2,1,0:T(8,128)(2,1)S(1)} collective-permute-done((bf16[2,192,256]{2,1,0:T(8,128)(2,1)S(1)}, bf16[2,192,256]{2,1,0:T(8,128)(2,1)S(1)}, u32[]{:S(2)}, u32[]{:S(2)}) %collective-permute-start) | collective-permute-done | bytes 196640 | tf_op jit(solution)/shard_map/while/body/eval_jaxpr/ppermute | solution.py:12
  35.8 1.9 collective-permute-start
  37.8 8.4 %collective-permute-done = bf16[2,192,256]{2,1,0:T(8,128)(2,1)S(1)} collective-permute-done((bf16[2,192,256]{2,1,0:T(8,128)(2,1)S(1)}, bf16[2,192,256]{2,1,0:T(8,128)(2,1)S(1)}, u32[]{:S(2)}, u32[]{:S(2)}) %collective-permute-start) | collective-permute-done | bytes 196640 | tf_op jit(solution)/shard_map/while/body/eval_jaxpr/ppermute | solution.py:12
  46.2 1.9 collective-permute-start
  48.1 8.4 %collective-permute-done = bf16[2,192,256]{2,1,0:T(8,128)(2,1)S(1)} collective-permute-done((bf16[2,192,256]{2,1,0:T(8,128)(2,1)S(1)}, bf16[2,192,256]{2,1,0:T(8,128)(2,1)S(1)}, u32[]{:S(2)}, u32[]{:S(2)}) %collective-permute-start) | collective-permute-done | bytes 196640 | tf_op jit(solution)/shard_map/while/body/eval_jaxpr/ppermute | solution.py:12
  56.6 1.9 collective-permute-start
  58.5 8.4 %collective-permute-done = bf16[2,192,256]{2,1,0:T(8,128)(2,1)S(1)} collective-permute-done((bf16[2,192,256]{2,1,0:T(8,128)(2,1)S(1)}, bf16[2,192,256]{2,1,0:T(8,128)(2,1)S(1)}, u32[]{:S(2)}, u32[]{:S(2)}) %collective-permute-start) | collective-permute-done | bytes 196640 | tf_op jit(solution)/shard_map/while/body/eval_jaxpr/ppermute | solution.py:12
  66.9 1.9 collective-permute-start
  68.9 8.4 %collective-permute-done = bf16[2,192,256]{2,1,0:T(8,128)(2,1)S(1)} collective-permute-done((bf16[2,192,256]{2,1,0:T(8,128)(2,1)S(1)}, bf16[2,192,256]{2,1,0:T(8,128)(2,1)S(1)}, u32[]{:S(2)}, u32[]{:S(2)}) %collective-permute-start) | collective-permute-done | bytes 196640 | tf_op jit(solution)/shard_map/while/body/eval_jaxpr/ppermute | solution.py:12
  77.3 1.9 collective-permute-start
  79.2 8.4 %collective-permute-done = bf16[2,192,256]{2,1,0:T(8,128)(2,1)S(1)} collective-permute-done((bf16[2,192,256]{2,1,0:T(8,128)(2,1)S(1)}, bf16[2,192,256]{2,1,0:T(8,128)(2,1)S(1)}, u32[]{:S(2)}, u32[]{:S(2)}) %collective-permute-start) | collective-permute-done | bytes 196640 | tf_op jit(solution)/shard_map/while/body/eval_jaxpr/ppermute | solution.py:12
  87.7 1.9 collective-permute-start
  89.6 8.4 %collective-permute-done = bf16[2,192,256]{2,1,0:T(8,128)(2,1)S(1)} collective-permute-done((bf16[2,192,256]{2,1,0:T(8,128)(2,1)S(1)}, bf16[2,192,256]{2,1,0:T(8,128)(2,1)S(1)}, u32[]{:S(2)}, u32[]{:S(2)}) %collective-permute-start) | collective-permute-done | bytes 196640 | tf_op jit(solution)/shard_map/while/body/eval_jaxpr/ppermute | solution.py:12
  98.0 1.9 collective-permute-start
  100.0 8.4 %collective-permute-done = bf16[2,192,256]{2,1,0:T(8,128)(2,1)S(1)} collective-permute-done((bf16[2,192,256]{2,1,0:T(8,128)(2,1)S(1)}, bf16[2,192,256]{2,1,0:T(8,128)(2,1)S(1)}, u32[]{:S(2)}, u32[]{:S(2)}) %collective-permute-start) | collective-permute-done | bytes 196640 | tf_op jit(solution)/shard_map/while/body/eval_jaxpr/ppermute | solution.py:12
  108.4 1.9 collective-permute-start
  110.4 8.4 %collective-permute-done = bf16[2,192,256]{2,1,0:T(8,128)(2,1)S(1)} collective-permute-done((bf16[2,192,256]{2,1,0:T(8,128)(2,1)S(1)}, bf16[2,192,256]{2,1,0:T(8,128)(2,1)S(1)}, u32[]{:S(2)}, u32[]{:S(2)}) %collective-permute-start) | collective-permute-done | bytes 196640 | tf_op jit(solution)/shard_map/while/body/eval_jaxpr/ppermute | solution.py:12
  118.8 1.9 collective-permute-start
  120.7 8.4 %collective-permute-done = bf16[2,192,256]{2,1,0:T(8,128)(2,1)S(1)} collective-permute-done((bf16[2,192,256]{2,1,0:T(8,128)(2,1)S(1)}, bf16[2,192,256]{2,1,0:T(8,128)(2,1)S(1)}, u32[]{:S(2)}, u32[]{:S(2)}) %collective-permute-start) | collective-permute-done | bytes 196640 | tf_op jit(solution)/shard_map/while/body/eval_jaxpr/ppermute | solution.py:12
  129.2 1.9 collective-permute-start
  131.1 8.4 %collective-permute-done = bf16[2,192,256]{2,1,0:T(8,128)(2,1)S(1)} collective-permute-done((bf16[2,192,256]{2,1,0:T(8,128)(2,1)S(1)}, bf16[2,192,256]{2,1,0:T(8,128)(2,1)S(1)}, u32[]{:S(2)}, u32[]{:S(2)}) %collective-permute-start) | collective-permute-done | bytes 196640 | tf_op jit(solution)/shard_map/while/body/eval_jaxpr/ppermute | solution.py:12
  139.5 1.9 collective-permute-start
  141.5 8.4 %collective-permute-done = bf16[2,192,256]{2,1,0:T(8,128)(2,1)S(1)} collective-permute-done((bf16[2,192,256]{2,1,0:T(8,128)(2,1)S(1)}, bf16[2,192,256]{2,1,0:T(8,128)(2,1)S(1)}, u32[]{:S(2)}, u32[]{:S(2)}) %collective-permute-start) | collective-permute-done | bytes 196640 | tf_op jit(solution)/shard_map/while/body/eval_jaxpr/ppermute | solution.py:12
  149.9 1.9 collective-permute-start
  151.8 8.4 %collective-permute-done = bf16[2,192,256]{2,1,0:T(8,128)(2,1)S(1)} collective-permute-done((bf16[2,192,256]{2,1,0:T(8,128)(2,1)S(1)}, bf16[2,192,256]{2,1,0:T(8,128)(2,1)S(1)}, u32[]{:S(2)}, u32[]{:S(2)}) %collective-permute-start) | collective-permute-done | bytes 196640 | tf_op jit(solution)/shard_map/while/body/eval_jaxpr/ppermute | solution.py:12
  160.3 3.1 copy.21
  163.3 3.9 %fusion.51 = (bf16[1,3072,256]{1,2,0:T(8,128)(2,1)}, bf16[1,3072,256]{1,2,0:T(8,128)(2,1)}) fusion(bf16[2,3072,256]{1,2,0:T(8,128)(2,1)} %copy.21), kind=kLoop, calls=%fused_computation.39 | loop fusion | bytes 6291456 | tf_op jit(solution)/shard_map/slice | solution.py:64
  167.4 1.1 reshape.56
  168.6 143.1 %while.29 = (s32[]{:T(128)}, bf16[8,192,4,128]{3,1,2,0:T(8,128)(2,1)}, s32[8]{0:T(128)S(1)}, bf16[3072,2,128]{0,2,1:T(8,128)(2,1)}, bf16[3072,2,128]{0,2,1:T(8,1...) while((s32[]{:T(128)}, ...), condition=%wide.region_8.9_spmd.clone, body=%wide.region_5.8_spmd.clone.sunk | while | flops 1224084480 | bytes 13599102 | solution.py:73
  168.6 0.7 dynamic_slice.57
  174.0 7.8 %fusion.61 = (f32[4,192]{1,0:T(4,128)S(1)}, bf16[4,192,3072]{2,1,0:T(8,128)(2,1)}) fusion(pred[192,3072]{1,0:T(8,128)(4,1)S(1)} %compare_and_fusion.2, bf16[3072,2,128]{0,2,1:T(8,128)(2,1)} %get-tuple-element.393, s32[]{:T(128)S(6)} %select_n.75, bf16[1,192,4,128]{3,2,0,1:T(4,128)(2,1)S(1)} %constant_dynamic-slice_fusion.2), kind=kOutput, calls=%fused_computation.38.clone.1 | convolution fusion | flops 618138624 | bytes 6884356 | tf_op jit(solution)/shard_map/while/body/eval_jaxpr/sub | solution.py:21
  181.8 4.6 %fusion.62 = bf16[8,192,4,128]{3,1,2,0:T(8,128)(2,1)} fusion(bf16[8,192,4,128]{3,1,2,0:T(8,128)(2,1)} %get-tuple-element.374, s32[]{:T(128)} %get-tuple-element.373, bf16[4,192,3072]{2,1,0:T(8,128)(2,1)} %get-tuple-element.331, bf16[3072,2,128]{0,2,1:T(8,128)(2,1)} %get-tuple-element.392, s32[]{:T(128)S(6)} %select_n.75, f32[192,4]{0,1:T(4,128)S(1)} %bitcast.94), kind=kOutput, calls=%fused_computation.17.clone.1 | convolution fusion | flops 604176384 | bytes 5705220 | tf_op jit(solution)/shard_map/while/body/eval_jaxpr/hqk,kd->qhd/dot_general | solution.py:24
  186.5 0.7 dynamic_slice.57
  191.9 7.8 %fusion.61 = (f32[4,192]{1,0:T(4,128)S(1)}, bf16[4,192,3072]{2,1,0:T(8,128)(2,1)}) fusion(pred[192,3072]{1,0:T(8,128)(4,1)S(1)} %compare_and_fusion.2, bf16[3072,2,128]{0,2,1:T(8,128)(2,1)} %get-tuple-element.393, s32[]{:T(128)S(6)} %select_n.75, bf16[1,192,4,128]{3,2,0,1:T(4,128)(2,1)S(1)} %constant_dynamic-slice_fusion.2), kind=kOutput, calls=%fused_computation.38.clone.1 | convolution fusion | flops 618138624 | bytes 6884356 | tf_op jit(solution)/shard_map/while/body/eval_jaxpr/sub | solution.py:21
  199.7 4.6 %fusion.62 = bf16[8,192,4,128]{3,1,2,0:T(8,128)(2,1)} fusion(bf16[8,192,4,128]{3,1,2,0:T(8,128)(2,1)} %get-tuple-element.374, s32[]{:T(128)} %get-tuple-element.373, bf16[4,192,3072]{2,1,0:T(8,128)(2,1)} %get-tuple-element.331, bf16[3072,2,128]{0,2,1:T(8,128)(2,1)} %get-tuple-element.392, s32[]{:T(128)S(6)} %select_n.75, f32[192,4]{0,1:T(4,128)S(1)} %bitcast.94), kind=kOutput, calls=%fused_computation.17.clone.1 | convolution fusion | flops 604176384 | bytes 5705220 | tf_op jit(solution)/shard_map/while/body/eval_jaxpr/hqk,kd->qhd/dot_general | solution.py:24
  204.3 0.7 dynamic_slice.57
  209.8 7.8 %fusion.61 = (f32[4,192]{1,0:T(4,128)S(1)}, bf16[4,192,3072]{2,1,0:T(8,128)(2,1)}) fusion(pred[192,3072]{1,0:T(8,128)(4,1)S(1)} %compare_and_fusion.2, bf16[3072,2,128]{0,2,1:T(8,128)(2,1)} %get-tuple-element.393, s32[]{:T(128)S(6)} %select_n.75, bf16[1,192,4,128]{3,2,0,1:T(4,128)(2,1)S(1)} %constant_dynamic-slice_fusion.2), kind=kOutput, calls=%fused_computation.38.clone.1 | convolution fusion | flops 618138624 | bytes 6884356 | tf_op jit(solution)/shard_map/while/body/eval_jaxpr/sub | solution.py:21
  217.6 4.6 %fusion.62 = bf16[8,192,4,128]{3,1,2,0:T(8,128)(2,1)} fusion(bf16[8,192,4,128]{3,1,2,0:T(8,128)(2,1)} %get-tuple-element.374, s32[]{:T(128)} %get-tuple-element.373, bf16[4,192,3072]{2,1,0:T(8,128)(2,1)} %get-tuple-element.331, bf16[3072,2,128]{0,2,1:T(8,128)(2,1)} %get-tuple-element.392, s32[]{:T(128)S(6)} %select_n.75, f32[192,4]{0,1:T(4,128)S(1)} %bitcast.94), kind=kOutput, calls=%fused_computation.17.clone.1 | convolution fusion | flops 604176384 | bytes 5705220 | tf_op jit(solution)/shard_map/while/body/eval_jaxpr/hqk,kd->qhd/dot_general | solution.py:24
  222.2 0.7 dynamic_slice.57
  227.7 7.8 %fusion.61 = (f32[4,192]{1,0:T(4,128)S(1)}, bf16[4,192,3072]{2,1,0:T(8,128)(2,1)}) fusion(pred[192,3072]{1,0:T(8,128)(4,1)S(1)} %compare_and_fusion.2, bf16[3072,2,128]{0,2,1:T(8,128)(2,1)} %get-tuple-element.393, s32[]{:T(128)S(6)} %select_n.75, bf16[1,192,4,128]{3,2,0,1:T(4,128)(2,1)S(1)} %constant_dynamic-slice_fusion.2), kind=kOutput, calls=%fused_computation.38.clone.1 | convolution fusion | flops 618138624 | bytes 6884356 | tf_op jit(solution)/shard_map/while/body/eval_jaxpr/sub | solution.py:21
  235.5 4.6 %fusion.62 = bf16[8,192,4,128]{3,1,2,0:T(8,128)(2,1)} fusion(bf16[8,192,4,128]{3,1,2,0:T(8,128)(2,1)} %get-tuple-element.374, s32[]{:T(128)} %get-tuple-element.373, bf16[4,192,3072]{2,1,0:T(8,128)(2,1)} %get-tuple-element.331, bf16[3072,2,128]{0,2,1:T(8,128)(2,1)} %get-tuple-element.392, s32[]{:T(128)S(6)} %select_n.75, f32[192,4]{0,1:T(4,128)S(1)} %bitcast.94), kind=kOutput, calls=%fused_computation.17.clone.1 | convolution fusion | flops 604176384 | bytes 5705220 | tf_op jit(solution)/shard_map/while/body/eval_jaxpr/hqk,kd->qhd/dot_general | solution.py:24
  240.1 0.7 dynamic_slice.57
  245.6 7.8 %fusion.61 = (f32[4,192]{1,0:T(4,128)S(1)}, bf16[4,192,3072]{2,1,0:T(8,128)(2,1)}) fusion(pred[192,3072]{1,0:T(8,128)(4,1)S(1)} %compare_and_fusion.2, bf16[3072,2,128]{0,2,1:T(8,128)(2,1)} %get-tuple-element.393, s32[]{:T(128)S(6)} %select_n.75, bf16[1,192,4,128]{3,2,0,1:T(4,128)(2,1)S(1)} %constant_dynamic-slice_fusion.2), kind=kOutput, calls=%fused_computation.38.clone.1 | convolution fusion | flops 618138624 | bytes 6884356 | tf_op jit(solution)/shard_map/while/body/eval_jaxpr/sub | solution.py:21
  253.3 4.6 %fusion.62 = bf16[8,192,4,128]{3,1,2,0:T(8,128)(2,1)} fusion(bf16[8,192,4,128]{3,1,2,0:T(8,128)(2,1)} %get-tuple-element.374, s32[]{:T(128)} %get-tuple-element.373, bf16[4,192,3072]{2,1,0:T(8,128)(2,1)} %get-tuple-element.331, bf16[3072,2,128]{0,2,1:T(8,128)(2,1)} %get-tuple-element.392, s32[]{:T(128)S(6)} %select_n.75, f32[192,4]{0,1:T(4,128)S(1)} %bitcast.94), kind=kOutput, calls=%fused_computation.17.clone.1 | convolution fusion | flops 604176384 | bytes 5705220 | tf_op jit(solution)/shard_map/while/body/eval_jaxpr/hqk,kd->qhd/dot_general | solution.py:24
  258.0 0.7 dynamic_slice.57
  263.4 7.8 %fusion.61 = (f32[4,192]{1,0:T(4,128)S(1)}, bf16[4,192,3072]{2,1,0:T(8,128)(2,1)}) fusion(pred[192,3072]{1,0:T(8,128)(4,1)S(1)} %compare_and_fusion.2, bf16[3072,2,128]{0,2,1:T(8,128)(2,1)} %get-tuple-element.393, s32[]{:T(128)S(6)} %select_n.75, bf16[1,192,4,128]{3,2,0,1:T(4,128)(2,1)S(1)} %constant_dynamic-slice_fusion.2), kind=kOutput, calls=%fused_computation.38.clone.1 | convolution fusion | flops 618138624 | bytes 6884356 | tf_op jit(solution)/shard_map/while/body/eval_jaxpr/sub | solution.py:21
  271.2 4.6 %fusion.62 = bf16[8,192,4,128]{3,1,2,0:T(8,128)(2,1)} fusion(bf16[8,192,4,128]{3,1,2,0:T(8,128)(2,1)} %get-tuple-element.374, s32[]{:T(128)} %get-tuple-element.373, bf16[4,192,3072]{2,1,0:T(8,128)(2,1)} %get-tuple-element.331, bf16[3072,2,128]{0,2,1:T(8,128)(2,1)} %get-tuple-element.392, s32[]{:T(128)S(6)} %select_n.75, f32[192,4]{0,1:T(4,128)S(1)} %bitcast.94), kind=kOutput, calls=%fused_computation.17.clone.1 | convolution fusion | flops 604176384 | bytes 5705220 | tf_op jit(solution)/shard_map/while/body/eval_jaxpr/hqk,kd->qhd/dot_general | solution.py:24
  281.3 7.8 %fusion.61 = (f32[4,192]{1,0:T(4,128)S(1)}, bf16[4,192,3072]{2,1,0:T(8,128)(2,1)}) fusion(pred[192,3072]{1,0:T(8,128)(4,1)S(1)} %compare_and_fusion.2, bf16[3072,2,128]{0,2,1:T(8,128)(2,1)} %get-tuple-element.393, s32[]{:T(128)S(6)} %select_n.75, bf16[1,192,4,128]{3,2,0,1:T(4,128)(2,1)S(1)} %constant_dynamic-slice_fusion.2), kind=kOutput, calls=%fused_computation.38.clone.1 | convolution fusion | flops 618138624 | bytes 6884356 | tf_op jit(solution)/shard_map/while/body/eval_jaxpr/sub | solution.py:21
  289.1 4.6 %fusion.62 = bf16[8,192,4,128]{3,1,2,0:T(8,128)(2,1)} fusion(bf16[8,192,4,128]{3,1,2,0:T(8,128)(2,1)} %get-tuple-element.374, s32[]{:T(128)} %get-tuple-element.373, bf16[4,192,3072]{2,1,0:T(8,128)(2,1)} %get-tuple-element.331, bf16[3072,2,128]{0,2,1:T(8,128)(2,1)} %get-tuple-element.392, s32[]{:T(128)S(6)} %select_n.75, f32[192,4]{0,1:T(4,128)S(1)} %bitcast.94), kind=kOutput, calls=%fused_computation.17.clone.1 | convolution fusion | flops 604176384 | bytes 5705220 | tf_op jit(solution)/shard_map/while/body/eval_jaxpr/hqk,kd->qhd/dot_general | solution.py:24
  299.2 7.8 %fusion.61 = (f32[4,192]{1,0:T(4,128)S(1)}, bf16[4,192,3072]{2,1,0:T(8,128)(2,1)}) fusion(pred[192,3072]{1,0:T(8,128)(4,1)S(1)} %compare_and_fusion.2, bf16[3072,2,128]{0,2,1:T(8,128)(2,1)} %get-tuple-element.393, s32[]{:T(128)S(6)} %select_n.75, bf16[1,192,4,128]{3,2,0,1:T(4,128)(2,1)S(1)} %constant_dynamic-slice_fusion.2), kind=kOutput, calls=%fused_computation.38.clone.1 | convolution fusion | flops 618138624 | bytes 6884356 | tf_op jit(solution)/shard_map/while/body/eval_jaxpr/sub | solution.py:21
  307.0 4.6 %fusion.62 = bf16[8,192,4,128]{3,1,2,0:T(8,128)(2,1)} fusion(bf16[8,192,4,128]{3,1,2,0:T(8,128)(2,1)} %get-tuple-element.374, s32[]{:T(128)} %get-tuple-element.373, bf16[4,192,3072]{2,1,0:T(8,128)(2,1)} %get-tuple-element.331, bf16[3072,2,128]{0,2,1:T(8,128)(2,1)} %get-tuple-element.392, s32[]{:T(128)S(6)} %select_n.75, f32[192,4]{0,1:T(4,128)S(1)} %bitcast.94), kind=kOutput, calls=%fused_computation.17.clone.1 | convolution fusion | flops 604176384 | bytes 5705220 | tf_op jit(solution)/shard_map/while/body/eval_jaxpr/hqk,kd->qhd/dot_general | solution.py:24
  311.6 2.6 copy.27
  314.3 1.2 all_to_all.14
  315.5 18.2 %all_to_all.19 = bf16[4,48,4096]{2,1,0:T(8,128)(2,1)S(1)} all-to-all(bf16[4,48,4096]{2,1,0:T(8,128)(2,1)S(1)} %all_to_all.14), channel_id=1, replica_groups=mesh['ctx'=64,'head'=4] {'head'}, dimensions={0} | all-to-all | bytes 3145728 | tf_op jit(solution)/shard_map/all_to_all | solution.py:75
  333.7 1.2 copy.32
  (61 shorter events, 7.9 us)
Async XLA Ops:
  4.7 10.3 %collective-permute-start = (bf16[2,192,256]{2,1,0:T(8,128)(2,1)S(1)}, bf16[2,192,256]{2,1,0:T(8,128)(2,1)S(1)}, u32[]{:S(2)}, u32[]{:S(2)}) collective-permute-start(bf16[2,192,256]{2,1,0:T(8,128)(2,1)S(1)} %get-tuple-element.343), channel_id=1, source_target_pairs={{0,4},{4,8},{8,12},{12,16},{16,20},{20,24},{24,28},{28,32},{32,36}... | collective-permute-start | bytes 589832 | tf_op jit(solution)/shard_map/while/body/eval_jaxpr/ppermute | solution.py:12
  15.1 10.3 %collective-permute-start = (bf16[2,192,256]{2,1,0:T(8,128)(2,1)S(1)}, bf16[2,192,256]{2,1,0:T(8,128)(2,1)S(1)}, u32[]{:S(2)}, u32[]{:S(2)}) collective-permute-start(bf16[2,192,256]{2,1,0:T(8,128)(2,1)S(1)} %get-tuple-element.343), channel_id=1, source_target_pairs={{0,4},{4,8},{8,12},{12,16},{16,20},{20,24},{24,28},{28,32},{32,36}... | collective-permute-start | bytes 589832 | tf_op jit(solution)/shard_map/while/body/eval_jaxpr/ppermute | solution.py:12
  25.5 10.3 %collective-permute-start = (bf16[2,192,256]{2,1,0:T(8,128)(2,1)S(1)}, bf16[2,192,256]{2,1,0:T(8,128)(2,1)S(1)}, u32[]{:S(2)}, u32[]{:S(2)}) collective-permute-start(bf16[2,192,256]{2,1,0:T(8,128)(2,1)S(1)} %get-tuple-element.343), channel_id=1, source_target_pairs={{0,4},{4,8},{8,12},{12,16},{16,20},{20,24},{24,28},{28,32},{32,36}... | collective-permute-start | bytes 589832 | tf_op jit(solution)/shard_map/while/body/eval_jaxpr/ppermute | solution.py:12
  35.8 10.3 %collective-permute-start = (bf16[2,192,256]{2,1,0:T(8,128)(2,1)S(1)}, bf16[2,192,256]{2,1,0:T(8,128)(2,1)S(1)}, u32[]{:S(2)}, u32[]{:S(2)}) collective-permute-start(bf16[2,192,256]{2,1,0:T(8,128)(2,1)S(1)} %get-tuple-element.343), channel_id=1, source_target_pairs={{0,4},{4,8},{8,12},{12,16},{16,20},{20,24},{24,28},{28,32},{32,36}... | collective-permute-start | bytes 589832 | tf_op jit(solution)/shard_map/while/body/eval_jaxpr/ppermute | solution.py:12
  46.2 10.3 %collective-permute-start = (bf16[2,192,256]{2,1,0:T(8,128)(2,1)S(1)}, bf16[2,192,256]{2,1,0:T(8,128)(2,1)S(1)}, u32[]{:S(2)}, u32[]{:S(2)}) collective-permute-start(bf16[2,192,256]{2,1,0:T(8,128)(2,1)S(1)} %get-tuple-element.343), channel_id=1, source_target_pairs={{0,4},{4,8},{8,12},{12,16},{16,20},{20,24},{24,28},{28,32},{32,36}... | collective-permute-start | bytes 589832 | tf_op jit(solution)/shard_map/while/body/eval_jaxpr/ppermute | solution.py:12
  56.6 10.3 %collective-permute-start = (bf16[2,192,256]{2,1,0:T(8,128)(2,1)S(1)}, bf16[2,192,256]{2,1,0:T(8,128)(2,1)S(1)}, u32[]{:S(2)}, u32[]{:S(2)}) collective-permute-start(bf16[2,192,256]{2,1,0:T(8,128)(2,1)S(1)} %get-tuple-element.343), channel_id=1, source_target_pairs={{0,4},{4,8},{8,12},{12,16},{16,20},{20,24},{24,28},{28,32},{32,36}... | collective-permute-start | bytes 589832 | tf_op jit(solution)/shard_map/while/body/eval_jaxpr/ppermute | solution.py:12
  66.9 10.3 %collective-permute-start = (bf16[2,192,256]{2,1,0:T(8,128)(2,1)S(1)}, bf16[2,192,256]{2,1,0:T(8,128)(2,1)S(1)}, u32[]{:S(2)}, u32[]{:S(2)}) collective-permute-start(bf16[2,192,256]{2,1,0:T(8,128)(2,1)S(1)} %get-tuple-element.343), channel_id=1, source_target_pairs={{0,4},{4,8},{8,12},{12,16},{16,20},{20,24},{24,28},{28,32},{32,36}... | collective-permute-start | bytes 589832 | tf_op jit(solution)/shard_map/while/body/eval_jaxpr/ppermute | solution.py:12
  77.3 10.3 %collective-permute-start = (bf16[2,192,256]{2,1,0:T(8,128)(2,1)S(1)}, bf16[2,192,256]{2,1,0:T(8,128)(2,1)S(1)}, u32[]{:S(2)}, u32[]{:S(2)}) collective-permute-start(bf16[2,192,256]{2,1,0:T(8,128)(2,1)S(1)} %get-tuple-element.343), channel_id=1, source_target_pairs={{0,4},{4,8},{8,12},{12,16},{16,20},{20,24},{24,28},{28,32},{32,36}... | collective-permute-start | bytes 589832 | tf_op jit(solution)/shard_map/while/body/eval_jaxpr/ppermute | solution.py:12
  87.7 10.3 %collective-permute-start = (bf16[2,192,256]{2,1,0:T(8,128)(2,1)S(1)}, bf16[2,192,256]{2,1,0:T(8,128)(2,1)S(1)}, u32[]{:S(2)}, u32[]{:S(2)}) collective-permute-start(bf16[2,192,256]{2,1,0:T(8,128)(2,1)S(1)} %get-tuple-element.343), channel_id=1, source_target_pairs={{0,4},{4,8},{8,12},{12,16},{16,20},{20,24},{24,28},{28,32},{32,36}... | collective-permute-start | bytes 589832 | tf_op jit(solution)/shard_map/while/body/eval_jaxpr/ppermute | solution.py:12
  98.0 10.3 %collective-permute-start = (bf16[2,192,256]{2,1,0:T(8,128)(2,1)S(1)}, bf16[2,192,256]{2,1,0:T(8,128)(2,1)S(1)}, u32[]{:S(2)}, u32[]{:S(2)}) collective-permute-start(bf16[2,192,256]{2,1,0:T(8,128)(2,1)S(1)} %get-tuple-element.343), channel_id=1, source_target_pairs={{0,4},{4,8},{8,12},{12,16},{16,20},{20,24},{24,28},{28,32},{32,36}... | collective-permute-start | bytes 589832 | tf_op jit(solution)/shard_map/while/body/eval_jaxpr/ppermute | solution.py:12
  108.4 10.3 %collective-permute-start = (bf16[2,192,256]{2,1,0:T(8,128)(2,1)S(1)}, bf16[2,192,256]{2,1,0:T(8,128)(2,1)S(1)}, u32[]{:S(2)}, u32[]{:S(2)}) collective-permute-start(bf16[2,192,256]{2,1,0:T(8,128)(2,1)S(1)} %get-tuple-element.343), channel_id=1, source_target_pairs={{0,4},{4,8},{8,12},{12,16},{16,20},{20,24},{24,28},{28,32},{32,36}... | collective-permute-start | bytes 589832 | tf_op jit(solution)/shard_map/while/body/eval_jaxpr/ppermute | solution.py:12
  118.8 10.3 %collective-permute-start = (bf16[2,192,256]{2,1,0:T(8,128)(2,1)S(1)}, bf16[2,192,256]{2,1,0:T(8,128)(2,1)S(1)}, u32[]{:S(2)}, u32[]{:S(2)}) collective-permute-start(bf16[2,192,256]{2,1,0:T(8,128)(2,1)S(1)} %get-tuple-element.343), channel_id=1, source_target_pairs={{0,4},{4,8},{8,12},{12,16},{16,20},{20,24},{24,28},{28,32},{32,36}... | collective-permute-start | bytes 589832 | tf_op jit(solution)/shard_map/while/body/eval_jaxpr/ppermute | solution.py:12
  129.2 10.3 %collective-permute-start = (bf16[2,192,256]{2,1,0:T(8,128)(2,1)S(1)}, bf16[2,192,256]{2,1,0:T(8,128)(2,1)S(1)}, u32[]{:S(2)}, u32[]{:S(2)}) collective-permute-start(bf16[2,192,256]{2,1,0:T(8,128)(2,1)S(1)} %get-tuple-element.343), channel_id=1, source_target_pairs={{0,4},{4,8},{8,12},{12,16},{16,20},{20,24},{24,28},{28,32},{32,36}... | collective-permute-start | bytes 589832 | tf_op jit(solution)/shard_map/while/body/eval_jaxpr/ppermute | solution.py:12
  139.5 10.3 %collective-permute-start = (bf16[2,192,256]{2,1,0:T(8,128)(2,1)S(1)}, bf16[2,192,256]{2,1,0:T(8,128)(2,1)S(1)}, u32[]{:S(2)}, u32[]{:S(2)}) collective-permute-start(bf16[2,192,256]{2,1,0:T(8,128)(2,1)S(1)} %get-tuple-element.343), channel_id=1, source_target_pairs={{0,4},{4,8},{8,12},{12,16},{16,20},{20,24},{24,28},{28,32},{32,36}... | collective-permute-start | bytes 589832 | tf_op jit(solution)/shard_map/while/body/eval_jaxpr/ppermute | solution.py:12
  149.9 10.3 %collective-permute-start = (bf16[2,192,256]{2,1,0:T(8,128)(2,1)S(1)}, bf16[2,192,256]{2,1,0:T(8,128)(2,1)S(1)}, u32[]{:S(2)}, u32[]{:S(2)}) collective-permute-start(bf16[2,192,256]{2,1,0:T(8,128)(2,1)S(1)} %get-tuple-element.343), channel_id=1, source_target_pairs={{0,4},{4,8},{8,12},{12,16},{16,20},{20,24},{24,28},{28,32},{32,36}... | collective-permute-start | bytes 589832 | tf_op jit(solution)/shard_map/while/body/eval_jaxpr/ppermute | solution.py:12
  163.3 4.1 %copy-start = (bf16[192,4096]{1,0:T(8,128)(2,1)S(1)}, bf16[192,4096]{1,0:T(8,128)(2,1)}, u32[]{:S(2)}) copy-start(bf16[192,4096]{1,0:T(8,128)(2,1)} %param.8) | copy-start | bytes 4718596
  167.2 1.4 copy-start.1
where the time goes:
time: 336 us; the launch traced here: 335 us
  waiting for transfers between devices  126 us (38%)
  matrix products  99.5 us (30%)
  loops' own time  34.1 us (10%)
  starting transfers between devices  28.8 us (9%)
  local copies, waits for them, and re-layouts  20.6 us (6%)
  blocking collectives  18.2 us (5%)
  other arithmetic  8.1 us (2%)
    ppermute x15, waiting for transfers between devices, passed_along(): lax.ppermute(value, axis, [(source, source + steps) for source in range(l...  126 us
    sub x8, matrix products, attend_group(): probs = jnp.where(allowed[None], jnp.exp(scores - highest), 0.0)  62.3 us
    dot_general x8, matrix products, attend_group(): jnp.einsum('hqk,kd->qhd', rounded, value_part, preferred_element_type=jnp...  37.2 us
    another operation x1, loops' own time, per_device(): mixed = lax.map(one_item, jnp.arange(item_count, dtype=jnp.int32))  33.4 us
    ppermute x15, starting transfers between devices, passed_along(): lax.ppermute(value, axis, [(source, source + steps) for source in range(l...  28.8 us
    all_to_all x1, blocking collectives, per_device(): lax.all_to_all(mixed, 'head', split_axis=0, concat_axis=1, tiled=True)  18.2 us
  transfers between devices with their start and end apart: 15, of which 15 were waited for; matrix products, arithmetic and copies ran while one was open for 0% of the time, Pallas kernels for 0%

commit v1 on v0

--- a/solution.py
+++ b/solution.py
@@ -72,7 +72,10 @@
 
     mixed = lax.map(one_item, jnp.arange(item_count, dtype=jnp.int32))
     mixed = jnp.moveaxis(mixed, 0, 1).reshape(tok_rows, item_count * heads_item * HEAD_SIZE)
-    return lax.all_to_all(mixed, "head", split_axis=0, concat_axis=1, tiled=True)
+    return jnp.concatenate(
+        lax.all_to_all(jnp.stack(jnp.split(mixed, lax.axis_size("head"), axis=0)), "head", 0, 0),
+        axis=1,
+    )
 
 
 def solution(mesh):

time: 336 us -> 336 us (level)
  no operation moved by 1% of the time
where the time goes in v1:
time: 336 us; the launch traced here: 335 us
  waiting for transfers between devices  126 us (38%)
  matrix products  99.5 us (30%)
  loops' own time  34.1 us (10%)
  starting transfers between devices  28.8 us (9%)
  local copies, waits for them, and re-layouts  19.9 us (6%)
  blocking collectives  18.2 us (5%)
  other arithmetic  8.3 us (2%)
    ppermute x15, waiting for transfers between devices, passed_along(): lax.ppermute(value, axis, [(source, source + steps) for source in range(l...  126 us
    sub x8, matrix products, attend_group(): probs = jnp.where(allowed[None], jnp.exp(scores - highest), 0.0)  62.4 us
    dot_general x8, matrix products, attend_group(): jnp.einsum('hqk,kd->qhd', rounded, value_part, preferred_element_type=jnp...  37.2 us
    another operation x1, loops' own time, per_device(): mixed = lax.map(one_item, jnp.arange(item_count, dtype=jnp.int32))  33.4 us
    ppermute x15, starting transfers between devices, passed_along(): lax.ppermute(value, axis, [(source, source + steps) for source in range(l...  28.8 us
    all_to_all x1, blocking collectives, per_device(): lax.all_to_all(jnp.stack(jnp.split(mixed, lax.axis_size('head'), axis=0))...  18.2 us
  transfers between devices with their start and end apart: 15, of which 15 were waited for; matrix products, arithmetic and copies ran while one was open for 0% of the time, Pallas kernels for 0%

profile of v1, /device:TPU:128, one launch (start us, length us, event | category | flops | bytes accessed | tf_op | source)
XLA Modules:
  0.0 334.6 jit_solution(12332290125141505312)
XLA Ops:
  0.0 0.8 copy.29
  1.0 1.9 convert_reduce_fusion
  3.5 1.0 pad_maximum_fusion.1
  4.7 155.5 %while.28 = (s32[]{:T(128)}, bf16[2,3072,256]{2,1,0:T(8,128)(2,1)S(1)}, bf16[2,192,256]{2,1,0:T(8,128)(2,1)S(1)}, s32[]{:T(128)}, s32[]{:T(128)}, /*index=5*/s32[]{:T(128)}, s32[]{:T(128)}, s32[]{:T(128)}) while((s32[]{:T(128)}, bf16[2,3072,256]{2,1,0:T(8,128)(2,1)S(1)}, bf16[2,192,256]{2,1,0:T(8,128)(2,1)S(1)}, s32[]{:T(128)}, s32[]{:T(128)}, ...), condition=%wide.region_1.0_spmd, body=%wide.region_0.0_spmd.sunk | while | flops 7 | bytes 1573051 | solution.py:50
  4.7 1.9 collective-permute-start
  6.7 8.4 %collective-permute-done = bf16[2,192,256]{2,1,0:T(8,128)(2,1)S(1)} collective-permute-done((bf16[2,192,256]{2,1,0:T(8,128)(2,1)S(1)}, bf16[2,192,256]{2,1,0:T(8,128)(2,1)S(1)}, u32[]{:S(2)}, u32[]{:S(2)}) %collective-permute-start) | collective-permute-done | bytes 196640 | tf_op jit(solution)/shard_map/while/body/eval_jaxpr/ppermute | solution.py:12
  15.1 1.9 collective-permute-start
  17.0 8.4 %collective-permute-done = bf16[2,192,256]{2,1,0:T(8,128)(2,1)S(1)} collective-permute-done((bf16[2,192,256]{2,1,0:T(8,128)(2,1)S(1)}, bf16[2,192,256]{2,1,0:T(8,128)(2,1)S(1)}, u32[]{:S(2)}, u32[]{:S(2)}) %collective-permute-start) | collective-permute-done | bytes 196640 | tf_op jit(solution)/shard_map/while/body/eval_jaxpr/ppermute | solution.py:12
  25.5 1.9 collective-permute-start
  27.4 8.4 %collective-permute-done = bf16[2,192,256]{2,1,0:T(8,128)(2,1)S(1)} collective-permute-done((bf16[2,192,256]{2,1,0:T(8,128)(2,1)S(1)}, bf16[2,192,256]{2,1,0:T(8,128)(2,1)S(1)}, u32[]{:S(2)}, u32[]{:S(2)}) %collective-permute-start) | collective-permute-done | bytes 196640 | tf_op jit(solution)/shard_map/while/body/eval_jaxpr/ppermute | solution.py:12
  35.8 1.9 collective-permute-start
  37.8 8.4 %collective-permute-done = bf16[2,192,256]{2,1,0:T(8,128)(2,1)S(1)} collective-permute-done((bf16[2,192,256]{2,1,0:T(8,128)(2,1)S(1)}, bf16[2,192,256]{2,1,0:T(8,128)(2,1)S(1)}, u32[]{:S(2)}, u32[]{:S(2)}) %collective-permute-start) | collective-permute-done | bytes 196640 | tf_op jit(solution)/shard_map/while/body/eval_jaxpr/ppermute | solution.py:12
  46.2 1.9 collective-permute-start
  48.1 8.4 %collective-permute-done = bf16[2,192,256]{2,1,0:T(8,128)(2,1)S(1)} collective-permute-done((bf16[2,192,256]{2,1,0:T(8,128)(2,1)S(1)}, bf16[2,192,256]{2,1,0:T(8,128)(2,1)S(1)}, u32[]{:S(2)}, u32[]{:S(2)}) %collective-permute-start) | collective-permute-done | bytes 196640 | tf_op jit(solution)/shard_map/while/body/eval_jaxpr/ppermute | solution.py:12
  56.6 1.9 collective-permute-start
  58.5 8.4 %collective-permute-done = bf16[2,192,256]{2,1,0:T(8,128)(2,1)S(1)} collective-permute-done((bf16[2,192,256]{2,1,0:T(8,128)(2,1)S(1)}, bf16[2,192,256]{2,1,0:T(8,128)(2,1)S(1)}, u32[]{:S(2)}, u32[]{:S(2)}) %collective-permute-start) | collective-permute-done | bytes 196640 | tf_op jit(solution)/shard_map/while/body/eval_jaxpr/ppermute | solution.py:12
  66.9 1.9 collective-permute-start
  68.9 8.4 %collective-permute-done = bf16[2,192,256]{2,1,0:T(8,128)(2,1)S(1)} collective-permute-done((bf16[2,192,256]{2,1,0:T(8,128)(2,1)S(1)}, bf16[2,192,256]{2,1,0:T(8,128)(2,1)S(1)}, u32[]{:S(2)}, u32[]{:S(2)}) %collective-permute-start) | collective-permute-done | bytes 196640 | tf_op jit(solution)/shard_map/while/body/eval_jaxpr/ppermute | solution.py:12
  77.3 1.9 collective-permute-start
  79.2 8.4 %collective-permute-done = bf16[2,192,256]{2,1,0:T(8,128)(2,1)S(1)} collective-permute-done((bf16[2,192,256]{2,1,0:T(8,128)(2,1)S(1)}, bf16[2,192,256]{2,1,0:T(8,128)(2,1)S(1)}, u32[]{:S(2)}, u32[]{:S(2)}) %collective-permute-start) | collective-permute-done | bytes 196640 | tf_op jit(solution)/shard_map/while/body/eval_jaxpr/ppermute | solution.py:12
  87.7 1.9 collective-permute-start
  89.6 8.4 %collective-permute-done = bf16[2,192,256]{2,1,0:T(8,128)(2,1)S(1)} collective-permute-done((bf16[2,192,256]{2,1,0:T(8,128)(2,1)S(1)}, bf16[2,192,256]{2,1,0:T(8,128)(2,1)S(1)}, u32[]{:S(2)}, u32[]{:S(2)}) %collective-permute-start) | collective-permute-done | bytes 196640 | tf_op jit(solution)/shard_map/while/body/eval_jaxpr/ppermute | solution.py:12
  98.0 1.9 collective-permute-start
  100.0 8.4 %collective-permute-done = bf16[2,192,256]{2,1,0:T(8,128)(2,1)S(1)} collective-permute-done((bf16[2,192,256]{2,1,0:T(8,128)(2,1)S(1)}, bf16[2,192,256]{2,1,0:T(8,128)(2,1)S(1)}, u32[]{:S(2)}, u32[]{:S(2)}) %collective-permute-start) | collective-permute-done | bytes 196640 | tf_op jit(solution)/shard_map/while/body/eval_jaxpr/ppermute | solution.py:12
  108.4 1.9 collective-permute-start
  110.4 8.4 %collective-permute-done = bf16[2,192,256]{2,1,0:T(8,128)(2,1)S(1)} collective-permute-done((bf16[2,192,256]{2,1,0:T(8,128)(2,1)S(1)}, bf16[2,192,256]{2,1,0:T(8,128)(2,1)S(1)}, u32[]{:S(2)}, u32[]{:S(2)}) %collective-permute-start) | collective-permute-done | bytes 196640 | tf_op jit(solution)/shard_map/while/body/eval_jaxpr/ppermute | solution.py:12
  118.8 1.9 collective-permute-start
  120.7 8.4 %collective-permute-done = bf16[2,192,256]{2,1,0:T(8,128)(2,1)S(1)} collective-permute-done((bf16[2,192,256]{2,1,0:T(8,128)(2,1)S(1)}, bf16[2,192,256]{2,1,0:T(8,128)(2,1)S(1)}, u32[]{:S(2)}, u32[]{:S(2)}) %collective-permute-start) | collective-permute-done | bytes 196640 | tf_op jit(solution)/shard_map/while/body/eval_jaxpr/ppermute | solution.py:12
  129.2 1.9 collective-permute-start
  131.1 8.4 %collective-permute-done = bf16[2,192,256]{2,1,0:T(8,128)(2,1)S(1)} collective-permute-done((bf16[2,192,256]{2,1,0:T(8,128)(2,1)S(1)}, bf16[2,192,256]{2,1,0:T(8,128)(2,1)S(1)}, u32[]{:S(2)}, u32[]{:S(2)}) %collective-permute-start) | collective-permute-done | bytes 196640 | tf_op jit(solution)/shard_map/while/body/eval_jaxpr/ppermute | solution.py:12
  139.5 1.9 collective-permute-start
  141.5 8.4 %collective-permute-done = bf16[2,192,256]{2,1,0:T(8,128)(2,1)S(1)} collective-permute-done((bf16[2,192,256]{2,1,0:T(8,128)(2,1)S(1)}, bf16[2,192,256]{2,1,0:T(8,128)(2,1)S(1)}, u32[]{:S(2)}, u32[]{:S(2)}) %collective-permute-start) | collective-permute-done | bytes 196640 | tf_op jit(solution)/shard_map/while/body/eval_jaxpr/ppermute | solution.py:12
  149.9 1.9 collective-permute-start
  151.8 8.4 %collective-permute-done = bf16[2,192,256]{2,1,0:T(8,128)(2,1)S(1)} collective-permute-done((bf16[2,192,256]{2,1,0:T(8,128)(2,1)S(1)}, bf16[2,192,256]{2,1,0:T(8,128)(2,1)S(1)}, u32[]{:S(2)}, u32[]{:S(2)}) %collective-permute-start) | collective-permute-done | bytes 196640 | tf_op jit(solution)/shard_map/while/body/eval_jaxpr/ppermute | solution.py:12
  160.3 3.1 copy.27
  163.3 3.9 %fusion.51 = (bf16[1,3072,256]{1,2,0:T(8,128)(2,1)}, bf16[1,3072,256]{1,2,0:T(8,128)(2,1)}) fusion(bf16[2,3072,256]{1,2,0:T(8,128)(2,1)} %copy.27), kind=kLoop, calls=%fused_computation.40 | loop fusion | bytes 6291456 | tf_op jit(solution)/shard_map/slice | solution.py:64
  167.4 1.1 reshape.66
  168.6 143.1 %while.29 = (s32[]{:T(128)}, bf16[8,192,4,128]{3,1,2,0:T(8,128)(2,1)}, s32[8]{0:T(128)S(1)}, bf16[3072,2,128]{0,2,1:T(8,128)(2,1)}, bf16[3072,2,128]{0,2,1:T(8,1...) while((s32[]{:T(128)}, ...), condition=%wide.region_8.9_spmd.clone, body=%wide.region_5.8_spmd.clone.sunk | while | flops 1224084480 | bytes 13599102 | solution.py:73
  168.6 0.7 dynamic_slice.57
  174.0 7.8 %fusion.62 = (f32[4,192]{1,0:T(4,128)S(1)}, bf16[4,192,3072]{2,1,0:T(8,128)(2,1)}) fusion(pred[192,3072]{1,0:T(8,128)(4,1)S(1)} %compare_and_fusion.2, bf16[3072,2,128]{0,2,1:T(8,128)(2,1)} %get-tuple-element.397, s32[]{:T(128)S(6)} %select_n.75, bf16[1,192,4,128]{3,2,0,1:T(4,128)(2,1)S(1)} %constant_dynamic-slice_fusion.2), kind=kOutput, calls=%fused_computation.39.clone.1 | convolution fusion | flops 618138624 | bytes 6884356 | tf_op jit(solution)/shard_map/while/body/eval_jaxpr/sub | solution.py:21
  181.8 4.6 %fusion.63 = bf16[8,192,4,128]{3,1,2,0:T(8,128)(2,1)} fusion(bf16[8,192,4,128]{3,1,2,0:T(8,128)(2,1)} %get-tuple-element.378, s32[]{:T(128)} %get-tuple-element.377, bf16[4,192,3072]{2,1,0:T(8,128)(2,1)} %get-tuple-element.335, bf16[3072,2,128]{0,2,1:T(8,128)(2,1)} %get-tuple-element.396, s32[]{:T(128)S(6)} %select_n.75, f32[192,4]{0,1:T(4,128)S(1)} %bitcast.94), kind=kOutput, calls=%fused_computation.17.clone.1 | convolution fusion | flops 604176384 | bytes 5705220 | tf_op jit(solution)/shard_map/while/body/eval_jaxpr/hqk,kd->qhd/dot_general | solution.py:24
  186.5 0.7 dynamic_slice.57
  191.9 7.8 %fusion.62 = (f32[4,192]{1,0:T(4,128)S(1)}, bf16[4,192,3072]{2,1,0:T(8,128)(2,1)}) fusion(pred[192,3072]{1,0:T(8,128)(4,1)S(1)} %compare_and_fusion.2, bf16[3072,2,128]{0,2,1:T(8,128)(2,1)} %get-tuple-element.397, s32[]{:T(128)S(6)} %select_n.75, bf16[1,192,4,128]{3,2,0,1:T(4,128)(2,1)S(1)} %constant_dynamic-slice_fusion.2), kind=kOutput, calls=%fused_computation.39.clone.1 | convolution fusion | flops 618138624 | bytes 6884356 | tf_op jit(solution)/shard_map/while/body/eval_jaxpr/sub | solution.py:21
  199.7 4.6 %fusion.63 = bf16[8,192,4,128]{3,1,2,0:T(8,128)(2,1)} fusion(bf16[8,192,4,128]{3,1,2,0:T(8,128)(2,1)} %get-tuple-element.378, s32[]{:T(128)} %get-tuple-element.377, bf16[4,192,3072]{2,1,0:T(8,128)(2,1)} %get-tuple-element.335, bf16[3072,2,128]{0,2,1:T(8,128)(2,1)} %get-tuple-element.396, s32[]{:T(128)S(6)} %select_n.75, f32[192,4]{0,1:T(4,128)S(1)} %bitcast.94), kind=kOutput, calls=%fused_computation.17.clone.1 | convolution fusion | flops 604176384 | bytes 5705220 | tf_op jit(solution)/shard_map/while/body/eval_jaxpr/hqk,kd->qhd/dot_general | solution.py:24
  204.4 0.7 dynamic_slice.57
  209.8 7.8 %fusion.62 = (f32[4,192]{1,0:T(4,128)S(1)}, bf16[4,192,3072]{2,1,0:T(8,128)(2,1)}) fusion(pred[192,3072]{1,0:T(8,128)(4,1)S(1)} %compare_and_fusion.2, bf16[3072,2,128]{0,2,1:T(8,128)(2,1)} %get-tuple-element.397, s32[]{:T(128)S(6)} %select_n.75, bf16[1,192,4,128]{3,2,0,1:T(4,128)(2,1)S(1)} %constant_dynamic-slice_fusion.2), kind=kOutput, calls=%fused_computation.39.clone.1 | convolution fusion | flops 618138624 | bytes 6884356 | tf_op jit(solution)/shard_map/while/body/eval_jaxpr/sub | solution.py:21
  217.6 4.6 %fusion.63 = bf16[8,192,4,128]{3,1,2,0:T(8,128)(2,1)} fusion(bf16[8,192,4,128]{3,1,2,0:T(8,128)(2,1)} %get-tuple-element.378, s32[]{:T(128)} %get-tuple-element.377, bf16[4,192,3072]{2,1,0:T(8,128)(2,1)} %get-tuple-element.335, bf16[3072,2,128]{0,2,1:T(8,128)(2,1)} %get-tuple-element.396, s32[]{:T(128)S(6)} %select_n.75, f32[192,4]{0,1:T(4,128)S(1)} %bitcast.94), kind=kOutput, calls=%fused_computation.17.clone.1 | convolution fusion | flops 604176384 | bytes 5705220 | tf_op jit(solution)/shard_map/while/body/eval_jaxpr/hqk,kd->qhd/dot_general | solution.py:24
  222.2 0.7 dynamic_slice.57
  227.7 7.8 %fusion.62 = (f32[4,192]{1,0:T(4,128)S(1)}, bf16[4,192,3072]{2,1,0:T(8,128)(2,1)}) fusion(pred[192,3072]{1,0:T(8,128)(4,1)S(1)} %compare_and_fusion.2, bf16[3072,2,128]{0,2,1:T(8,128)(2,1)} %get-tuple-element.397, s32[]{:T(128)S(6)} %select_n.75, bf16[1,192,4,128]{3,2,0,1:T(4,128)(2,1)S(1)} %constant_dynamic-slice_fusion.2), kind=kOutput, calls=%fused_computation.39.clone.1 | convolution fusion | flops 618138624 | bytes 6884356 | tf_op jit(solution)/shard_map/while/body/eval_jaxpr/sub | solution.py:21
  235.5 4.6 %fusion.63 = bf16[8,192,4,128]{3,1,2,0:T(8,128)(2,1)} fusion(bf16[8,192,4,128]{3,1,2,0:T(8,128)(2,1)} %get-tuple-element.378, s32[]{:T(128)} %get-tuple-element.377, bf16[4,192,3072]{2,1,0:T(8,128)(2,1)} %get-tuple-element.335, bf16[3072,2,128]{0,2,1:T(8,128)(2,1)} %get-tuple-element.396, s32[]{:T(128)S(6)} %select_n.75, f32[192,4]{0,1:T(4,128)S(1)} %bitcast.94), kind=kOutput, calls=%fused_computation.17.clone.1 | convolution fusion | flops 604176384 | bytes 5705220 | tf_op jit(solution)/shard_map/while/body/eval_jaxpr/hqk,kd->qhd/dot_general | solution.py:24
  240.1 0.7 dynamic_slice.57
  245.6 7.8 %fusion.62 = (f32[4,192]{1,0:T(4,128)S(1)}, bf16[4,192,3072]{2,1,0:T(8,128)(2,1)}) fusion(pred[192,3072]{1,0:T(8,128)(4,1)S(1)} %compare_and_fusion.2, bf16[3072,2,128]{0,2,1:T(8,128)(2,1)} %get-tuple-element.397, s32[]{:T(128)S(6)} %select_n.75, bf16[1,192,4,128]{3,2,0,1:T(4,128)(2,1)S(1)} %constant_dynamic-slice_fusion.2), kind=kOutput, calls=%fused_computation.39.clone.1 | convolution fusion | flops 618138624 | bytes 6884356 | tf_op jit(solution)/shard_map/while/body/eval_jaxpr/sub | solution.py:21
  253.4 4.6 %fusion.63 = bf16[8,192,4,128]{3,1,2,0:T(8,128)(2,1)} fusion(bf16[8,192,4,128]{3,1,2,0:T(8,128)(2,1)} %get-tuple-element.378, s32[]{:T(128)} %get-tuple-element.377, bf16[4,192,3072]{2,1,0:T(8,128)(2,1)} %get-tuple-element.335, bf16[3072,2,128]{0,2,1:T(8,128)(2,1)} %get-tuple-element.396, s32[]{:T(128)S(6)} %select_n.75, f32[192,4]{0,1:T(4,128)S(1)} %bitcast.94), kind=kOutput, calls=%fused_computation.17.clone.1 | convolution fusion | flops 604176384 | bytes 5705220 | tf_op jit(solution)/shard_map/while/body/eval_jaxpr/hqk,kd->qhd/dot_general | solution.py:24
  258.0 0.7 dynamic_slice.57
  263.5 7.8 %fusion.62 = (f32[4,192]{1,0:T(4,128)S(1)}, bf16[4,192,3072]{2,1,0:T(8,128)(2,1)}) fusion(pred[192,3072]{1,0:T(8,128)(4,1)S(1)} %compare_and_fusion.2, bf16[3072,2,128]{0,2,1:T(8,128)(2,1)} %get-tuple-element.397, s32[]{:T(128)S(6)} %select_n.75, bf16[1,192,4,128]{3,2,0,1:T(4,128)(2,1)S(1)} %constant_dynamic-slice_fusion.2), kind=kOutput, calls=%fused_computation.39.clone.1 | convolution fusion | flops 618138624 | bytes 6884356 | tf_op jit(solution)/shard_map/while/body/eval_jaxpr/sub | solution.py:21
  271.3 4.6 %fusion.63 = bf16[8,192,4,128]{3,1,2,0:T(8,128)(2,1)} fusion(bf16[8,192,4,128]{3,1,2,0:T(8,128)(2,1)} %get-tuple-element.378, s32[]{:T(128)} %get-tuple-element.377, bf16[4,192,3072]{2,1,0:T(8,128)(2,1)} %get-tuple-element.335, bf16[3072,2,128]{0,2,1:T(8,128)(2,1)} %get-tuple-element.396, s32[]{:T(128)S(6)} %select_n.75, f32[192,4]{0,1:T(4,128)S(1)} %bitcast.94), kind=kOutput, calls=%fused_computation.17.clone.1 | convolution fusion | flops 604176384 | bytes 5705220 | tf_op jit(solution)/shard_map/while/body/eval_jaxpr/hqk,kd->qhd/dot_general | solution.py:24
  275.9 0.7 dynamic_slice.57
  281.3 7.8 %fusion.62 = (f32[4,192]{1,0:T(4,128)S(1)}, bf16[4,192,3072]{2,1,0:T(8,128)(2,1)}) fusion(pred[192,3072]{1,0:T(8,128)(4,1)S(1)} %compare_and_fusion.2, bf16[3072,2,128]{0,2,1:T(8,128)(2,1)} %get-tuple-element.397, s32[]{:T(128)S(6)} %select_n.75, bf16[1,192,4,128]{3,2,0,1:T(4,128)(2,1)S(1)} %constant_dynamic-slice_fusion.2), kind=kOutput, calls=%fused_computation.39.clone.1 | convolution fusion | flops 618138624 | bytes 6884356 | tf_op jit(solution)/shard_map/while/body/eval_jaxpr/sub | solution.py:21
  289.1 4.6 %fusion.63 = bf16[8,192,4,128]{3,1,2,0:T(8,128)(2,1)} fusion(bf16[8,192,4,128]{3,1,2,0:T(8,128)(2,1)} %get-tuple-element.378, s32[]{:T(128)} %get-tuple-element.377, bf16[4,192,3072]{2,1,0:T(8,128)(2,1)} %get-tuple-element.335, bf16[3072,2,128]{0,2,1:T(8,128)(2,1)} %get-tuple-element.396, s32[]{:T(128)S(6)} %select_n.75, f32[192,4]{0,1:T(4,128)S(1)} %bitcast.94), kind=kOutput, calls=%fused_computation.17.clone.1 | convolution fusion | flops 604176384 | bytes 5705220 | tf_op jit(solution)/shard_map/while/body/eval_jaxpr/hqk,kd->qhd/dot_general | solution.py:24
  299.2 7.8 %fusion.62 = (f32[4,192]{1,0:T(4,128)S(1)}, bf16[4,192,3072]{2,1,0:T(8,128)(2,1)}) fusion(pred[192,3072]{1,0:T(8,128)(4,1)S(1)} %compare_and_fusion.2, bf16[3072,2,128]{0,2,1:T(8,128)(2,1)} %get-tuple-element.397, s32[]{:T(128)S(6)} %select_n.75, bf16[1,192,4,128]{3,2,0,1:T(4,128)(2,1)S(1)} %constant_dynamic-slice_fusion.2), kind=kOutput, calls=%fused_computation.39.clone.1 | convolution fusion | flops 618138624 | bytes 6884356 | tf_op jit(solution)/shard_map/while/body/eval_jaxpr/sub | solution.py:21
  307.0 4.6 %fusion.63 = bf16[8,192,4,128]{3,1,2,0:T(8,128)(2,1)} fusion(bf16[8,192,4,128]{3,1,2,0:T(8,128)(2,1)} %get-tuple-element.378, s32[]{:T(128)} %get-tuple-element.377, bf16[4,192,3072]{2,1,0:T(8,128)(2,1)} %get-tuple-element.335, bf16[3072,2,128]{0,2,1:T(8,128)(2,1)} %get-tuple-element.396, s32[]{:T(128)S(6)} %select_n.75, f32[192,4]{0,1:T(4,128)S(1)} %bitcast.94), kind=kOutput, calls=%fused_computation.17.clone.1 | convolution fusion | flops 604176384 | bytes 5705220 | tf_op jit(solution)/shard_map/while/body/eval_jaxpr/hqk,kd->qhd/dot_general | solution.py:24
  311.7 1.5 fusion.52
  315.2 18.2 %all_to_all.5 = bf16[4,48,4096]{2,1,0:T(8,128)(2,1)S(1)} all-to-all(bf16[4,48,4096]{2,1,0:T(8,128)(2,1)S(1)} %pad_maximum_fusion), channel_id=1, replica_groups=mesh['ctx'=64,'head'=4] {'head'}, dimensions={0} | all-to-all | bytes 3145728 | tf_op jit(solution)/shard_map/all_to_all | solution.py:76
  333.3 1.2 copy.41
  (69 shorter events, 9.2 us)
Async XLA Ops:
  4.7 10.3 %collective-permute-start = (bf16[2,192,256]{2,1,0:T(8,128)(2,1)S(1)}, bf16[2,192,256]{2,1,0:T(8,128)(2,1)S(1)}, u32[]{:S(2)}, u32[]{:S(2)}) collective-permute-start(bf16[2,192,256]{2,1,0:T(8,128)(2,1)S(1)} %get-tuple-element.347), channel_id=1, source_target_pairs={{0,4},{4,8},{8,12},{12,16},{16,20},{20,24},{24,28},{28,32},{32,36}... | collective-permute-start | bytes 589832 | tf_op jit(solution)/shard_map/while/body/eval_jaxpr/ppermute | solution.py:12
  15.1 10.3 %collective-permute-start = (bf16[2,192,256]{2,1,0:T(8,128)(2,1)S(1)}, bf16[2,192,256]{2,1,0:T(8,128)(2,1)S(1)}, u32[]{:S(2)}, u32[]{:S(2)}) collective-permute-start(bf16[2,192,256]{2,1,0:T(8,128)(2,1)S(1)} %get-tuple-element.347), channel_id=1, source_target_pairs={{0,4},{4,8},{8,12},{12,16},{16,20},{20,24},{24,28},{28,32},{32,36}... | collective-permute-start | bytes 589832 | tf_op jit(solution)/shard_map/while/body/eval_jaxpr/ppermute | solution.py:12
  25.5 10.3 %collective-permute-start = (bf16[2,192,256]{2,1,0:T(8,128)(2,1)S(1)}, bf16[2,192,256]{2,1,0:T(8,128)(2,1)S(1)}, u32[]{:S(2)}, u32[]{:S(2)}) collective-permute-start(bf16[2,192,256]{2,1,0:T(8,128)(2,1)S(1)} %get-tuple-element.347), channel_id=1, source_target_pairs={{0,4},{4,8},{8,12},{12,16},{16,20},{20,24},{24,28},{28,32},{32,36}... | collective-permute-start | bytes 589832 | tf_op jit(solution)/shard_map/while/body/eval_jaxpr/ppermute | solution.py:12
  35.8 10.3 %collective-permute-start = (bf16[2,192,256]{2,1,0:T(8,128)(2,1)S(1)}, bf16[2,192,256]{2,1,0:T(8,128)(2,1)S(1)}, u32[]{:S(2)}, u32[]{:S(2)}) collective-permute-start(bf16[2,192,256]{2,1,0:T(8,128)(2,1)S(1)} %get-tuple-element.347), channel_id=1, source_target_pairs={{0,4},{4,8},{8,12},{12,16},{16,20},{20,24},{24,28},{28,32},{32,36}... | collective-permute-start | bytes 589832 | tf_op jit(solution)/shard_map/while/body/eval_jaxpr/ppermute | solution.py:12
  46.2 10.3 %collective-permute-start = (bf16[2,192,256]{2,1,0:T(8,128)(2,1)S(1)}, bf16[2,192,256]{2,1,0:T(8,128)(2,1)S(1)}, u32[]{:S(2)}, u32[]{:S(2)}) collective-permute-start(bf16[2,192,256]{2,1,0:T(8,128)(2,1)S(1)} %get-tuple-element.347), channel_id=1, source_target_pairs={{0,4},{4,8},{8,12},{12,16},{16,20},{20,24},{24,28},{28,32},{32,36}... | collective-permute-start | bytes 589832 | tf_op jit(solution)/shard_map/while/body/eval_jaxpr/ppermute | solution.py:12
  56.6 10.3 %collective-permute-start = (bf16[2,192,256]{2,1,0:T(8,128)(2,1)S(1)}, bf16[2,192,256]{2,1,0:T(8,128)(2,1)S(1)}, u32[]{:S(2)}, u32[]{:S(2)}) collective-permute-start(bf16[2,192,256]{2,1,0:T(8,128)(2,1)S(1)} %get-tuple-element.347), channel_id=1, source_target_pairs={{0,4},{4,8},{8,12},{12,16},{16,20},{20,24},{24,28},{28,32},{32,36}... | collective-permute-start | bytes 589832 | tf_op jit(solution)/shard_map/while/body/eval_jaxpr/ppermute | solution.py:12
  66.9 10.3 %collective-permute-start = (bf16[2,192,256]{2,1,0:T(8,128)(2,1)S(1)}, bf16[2,192,256]{2,1,0:T(8,128)(2,1)S(1)}, u32[]{:S(2)}, u32[]{:S(2)}) collective-permute-start(bf16[2,192,256]{2,1,0:T(8,128)(2,1)S(1)} %get-tuple-element.347), channel_id=1, source_target_pairs={{0,4},{4,8},{8,12},{12,16},{16,20},{20,24},{24,28},{28,32},{32,36}... | collective-permute-start | bytes 589832 | tf_op jit(solution)/shard_map/while/body/eval_jaxpr/ppermute | solution.py:12
  77.3 10.3 %collective-permute-start = (bf16[2,192,256]{2,1,0:T(8,128)(2,1)S(1)}, bf16[2,192,256]{2,1,0:T(8,128)(2,1)S(1)}, u32[]{:S(2)}, u32[]{:S(2)}) collective-permute-start(bf16[2,192,256]{2,1,0:T(8,128)(2,1)S(1)} %get-tuple-element.347), channel_id=1, source_target_pairs={{0,4},{4,8},{8,12},{12,16},{16,20},{20,24},{24,28},{28,32},{32,36}... | collective-permute-start | bytes 589832 | tf_op jit(solution)/shard_map/while/body/eval_jaxpr/ppermute | solution.py:12
  87.7 10.3 %collective-permute-start = (bf16[2,192,256]{2,1,0:T(8,128)(2,1)S(1)}, bf16[2,192,256]{2,1,0:T(8,128)(2,1)S(1)}, u32[]{:S(2)}, u32[]{:S(2)}) collective-permute-start(bf16[2,192,256]{2,1,0:T(8,128)(2,1)S(1)} %get-tuple-element.347), channel_id=1, source_target_pairs={{0,4},{4,8},{8,12},{12,16},{16,20},{20,24},{24,28},{28,32},{32,36}... | collective-permute-start | bytes 589832 | tf_op jit(solution)/shard_map/while/body/eval_jaxpr/ppermute | solution.py:12
  98.0 10.3 %collective-permute-start = (bf16[2,192,256]{2,1,0:T(8,128)(2,1)S(1)}, bf16[2,192,256]{2,1,0:T(8,128)(2,1)S(1)}, u32[]{:S(2)}, u32[]{:S(2)}) collective-permute-start(bf16[2,192,256]{2,1,0:T(8,128)(2,1)S(1)} %get-tuple-element.347), channel_id=1, source_target_pairs={{0,4},{4,8},{8,12},{12,16},{16,20},{20,24},{24,28},{28,32},{32,36}... | collective-permute-start | bytes 589832 | tf_op jit(solution)/shard_map/while/body/eval_jaxpr/ppermute | solution.py:12
  108.4 10.3 %collective-permute-start = (bf16[2,192,256]{2,1,0:T(8,128)(2,1)S(1)}, bf16[2,192,256]{2,1,0:T(8,128)(2,1)S(1)}, u32[]{:S(2)}, u32[]{:S(2)}) collective-permute-start(bf16[2,192,256]{2,1,0:T(8,128)(2,1)S(1)} %get-tuple-element.347), channel_id=1, source_target_pairs={{0,4},{4,8},{8,12},{12,16},{16,20},{20,24},{24,28},{28,32},{32,36}... | collective-permute-start | bytes 589832 | tf_op jit(solution)/shard_map/while/body/eval_jaxpr/ppermute | solution.py:12
  118.8 10.3 %collective-permute-start = (bf16[2,192,256]{2,1,0:T(8,128)(2,1)S(1)}, bf16[2,192,256]{2,1,0:T(8,128)(2,1)S(1)}, u32[]{:S(2)}, u32[]{:S(2)}) collective-permute-start(bf16[2,192,256]{2,1,0:T(8,128)(2,1)S(1)} %get-tuple-element.347), channel_id=1, source_target_pairs={{0,4},{4,8},{8,12},{12,16},{16,20},{20,24},{24,28},{28,32},{32,36}... | collective-permute-start | bytes 589832 | tf_op jit(solution)/shard_map/while/body/eval_jaxpr/ppermute | solution.py:12
  129.2 10.3 %collective-permute-start = (bf16[2,192,256]{2,1,0:T(8,128)(2,1)S(1)}, bf16[2,192,256]{2,1,0:T(8,128)(2,1)S(1)}, u32[]{:S(2)}, u32[]{:S(2)}) collective-permute-start(bf16[2,192,256]{2,1,0:T(8,128)(2,1)S(1)} %get-tuple-element.347), channel_id=1, source_target_pairs={{0,4},{4,8},{8,12},{12,16},{16,20},{20,24},{24,28},{28,32},{32,36}... | collective-permute-start | bytes 589832 | tf_op jit(solution)/shard_map/while/body/eval_jaxpr/ppermute | solution.py:12
  139.5 10.3 %collective-permute-start = (bf16[2,192,256]{2,1,0:T(8,128)(2,1)S(1)}, bf16[2,192,256]{2,1,0:T(8,128)(2,1)S(1)}, u32[]{:S(2)}, u32[]{:S(2)}) collective-permute-start(bf16[2,192,256]{2,1,0:T(8,128)(2,1)S(1)} %get-tuple-element.347), channel_id=1, source_target_pairs={{0,4},{4,8},{8,12},{12,16},{16,20},{20,24},{24,28},{28,32},{32,36}... | collective-permute-start | bytes 589832 | tf_op jit(solution)/shard_map/while/body/eval_jaxpr/ppermute | solution.py:12
  149.9 10.3 %collective-permute-start = (bf16[2,192,256]{2,1,0:T(8,128)(2,1)S(1)}, bf16[2,192,256]{2,1,0:T(8,128)(2,1)S(1)}, u32[]{:S(2)}, u32[]{:S(2)}) collective-permute-start(bf16[2,192,256]{2,1,0:T(8,128)(2,1)S(1)} %get-tuple-element.347), channel_id=1, source_target_pairs={{0,4},{4,8},{8,12},{12,16},{16,20},{20,24},{24,28},{28,32},{32,36}... | collective-permute-start | bytes 589832 | tf_op jit(solution)/shard_map/while/body/eval_jaxpr/ppermute | solution.py:12
  163.3 4.1 %copy-start = (bf16[192,4096]{1,0:T(8,128)(2,1)S(1)}, bf16[192,4096]{1,0:T(8,128)(2,1)}, u32[]{:S(2)}) copy-start(bf16[192,4096]{1,0:T(8,128)(2,1)} %param.8) | copy-start | bytes 4718596
  167.4 1.2 copy-start.1
